TPU v7x, 32 devices: a whole 2x2x4 slice. The times are simulated.
32 devices in a mesh: wall: 4 (over y, x), gas: 8 (over z, core).
Axes of the slice: x: 2, y: 2, z: 4, core: 2. Of those that a mesh axis runs over, the one named last changes fastest.
Arguments:
- gas_state: float32 [3, 4, 512, 4096], P(None, None, 'wall', 'gas'), may hold values from -8 to 8
- wall_flags: int32 [512, 32], P('wall', 'gas'), may hold values from 0 to 128
- film_state: float32 [4, 512, 4096], P(None, 'wall', 'gas'), may hold values from -12 to 12, as said below
- deposit: float32 [512, 4096], P('wall', 'gas'), may hold values from 0.05 to 1
- owner_map: int32 [4, 8], replicated, may hold values from 0 to 7, each once within a row
Outputs:
- film_out: float32 [4, 512, 4096], P(None, ('wall', 'gas'))
- cfl: float32 [], replicated
Inputs may be any that keep to these rules, and one draw needn't show every extreme that they name: film_state[0] is positive. `owner_map`: each row is a permutation of 0 to 8 - 1.
All inputs are finite; a program needn't handle non-finite values.
Results may differ from a plain program's by a relative error of at most 0.00002.
Values sent between devices are 32-bit elements; how exact they have to be, the bound alone decides.
A program may use at most 64 MiB of HBM per device.

v0:
```python
import jax
import jax.numpy as jnp
from jax import lax
from jax.sharding import PartitionSpec as P

SUBSTEPS = 4


LAYER_WEIGHTS = (0.1, 0.2, 0.3, 0.4)
KAPPA = 0.41
HEIGHT_RATIO = 20.0
SPEED_FLOOR = 0.5
PRANDTL_TURB = 0.85
PRANDTL_JUMP = 3.0
LAMINAR_SHEAR = 0.3
LAMINAR_HEAT = 0.2
FILM_SPREAD = 0.24
FILM_FLOOR = 0.3
FRICTION = 0.5
GRAVITY = 1.0
COURANT = 6.0


def with_halo(value, sides, width):
    for axis, dim in sides:
        size, length = (lax.axis_size(axis), value.shape[dim])
        up = [(i, (i + 1) % size) for i in range(size)]
        down = [(j, i) for i, j in up]
        last = lax.slice_in_dim(value, length - width, length, axis=dim)
        leading = lax.slice_in_dim(value, 0, width, axis=dim)
        before = lax.ppermute(last, axis, up)
        after = lax.ppermute(leading, axis, down)
        value = jnp.concatenate([before, value, after], axis=dim)
    return value


def reichardt(scaled_height):
    return jnp.log1p(KAPPA * scaled_height) / KAPPA + 7.8 * (
        1.0 - jnp.exp(-scaled_height / 11.0) - scaled_height / 11.0 * jnp.exp(-scaled_height / 3.0)
    )


def surface_forcing(filtered, film_heat, attached, deposit):
    along, across, gas_heat = (filtered[0], filtered[1], filtered[2])
    wall_speed = jnp.sqrt(along * along + across * across + SPEED_FLOOR * SPEED_FLOOR)
    scaled_height = jnp.sqrt(HEIGHT_RATIO * wall_speed)
    scaled_speed = reichardt(scaled_height)
    factor = wall_speed / (scaled_speed * scaled_speed)
    contrast = gas_heat - film_heat
    shear_along = jnp.where(attached, factor * along, LAMINAR_SHEAR * along)
    shear_across = jnp.where(attached, factor * across, LAMINAR_SHEAR * across)
    heat_flux = jnp.where(
        attached,
        wall_speed * contrast / (PRANDTL_TURB * scaled_speed + PRANDTL_JUMP),
        LAMINAR_HEAT * contrast,
    )
    return jnp.stack([shear_along, shear_across, heat_flux, deposit])


def peak_speed(film_now):
    thickness = jnp.sqrt(film_now[0] * film_now[0] + FILM_FLOOR * FILM_FLOOR)
    moving = jnp.sqrt(film_now[1] * film_now[1] + film_now[2] * film_now[2])
    return jnp.max(moving / thickness + jnp.sqrt(GRAVITY * thickness))


def advance(padded, forcing, time_step):
    centre = padded[:, 1:-1, 1:-1]
    north_side = padded[:, :-2, 1:-1]
    south_side = padded[:, 2:, 1:-1]
    west_side = padded[:, 1:-1, :-2]
    east_side = padded[:, 1:-1, 2:]
    spread = north_side + south_side + west_side + east_side - 4.0 * centre
    height = centre[0]
    thickness = jnp.sqrt(height * height + FILM_FLOOR * FILM_FLOOR)
    divergence = 0.5 * (east_side[1] - west_side[1]) + 0.5 * (south_side[2] - north_side[2])
    slope_along = 0.5 * (east_side[0] - west_side[0])
    slope_across = 0.5 * (south_side[0] - north_side[0])
    new_height = height + FILM_SPREAD * spread[0] + time_step * (forcing[3] - divergence)
    new_along = (
        centre[1]
        + FILM_SPREAD * spread[1]
        + time_step
        * (forcing[0] - FRICTION * centre[1] / thickness - GRAVITY * height * slope_along)
    )
    new_across = (
        centre[2]
        + FILM_SPREAD * spread[2]
        + time_step
        * (forcing[1] - FRICTION * centre[2] / thickness - GRAVITY * height * slope_across)
    )
    new_heat = centre[3] + FILM_SPREAD * spread[3] + time_step * forcing[2] / thickness
    return jnp.stack([new_height, new_along, new_across, new_heat])


def per_device(gas_state, wall_flags, film_state, deposit, owner_map):
    tile_rows, tile_cols = (film_state.shape[1], film_state.shape[2])
    gas_count = lax.axis_size("gas")
    strip_rows = tile_rows // gas_count
    sampled = LAYER_WEIGHTS[0] * gas_state[:, 0]
    for layer in range(1, gas_state.shape[1]):
        sampled = sampled + LAYER_WEIGHTS[layer] * gas_state[:, layer]
    padded = with_halo(sampled, (("wall", 1), ("gas", 2)), 1)
    row_sum = padded[:, :-2] + padded[:, 1:-1] + padded[:, 2:]
    filtered = (row_sum[:, :, :-2] + row_sum[:, :, 1:-1] + row_sum[:, :, 2:]) / 9.0
    position = lax.broadcasted_iota(jnp.int32, (1, 1, 128), 2)
    attached = (position < wall_flags[:, :, None]).reshape(tile_rows, tile_cols)
    forcing = surface_forcing(filtered, film_state[3], attached, deposit)
    time_step = COURANT / lax.pmax(peak_speed(film_state), ("wall", "gas"))
    own_map = owner_map[lax.axis_index("wall")]
    slots = jnp.arange(gas_count, dtype=jnp.int32)
    inverse_row = jnp.sum(
        slots[None, :] * (own_map[None, :] == slots[:, None]).astype(jnp.int32), axis=1
    )
    film_now = film_state
    for substep in range(SUBSTEPS):
        beside_all = with_halo(film_now, (("wall", 1), ("gas", 2)), 1)
        film_now = advance(beside_all, forcing, time_step)
    divided = film_now.reshape(4, gas_count, strip_rows, tile_cols)
    pieces = divided[:, inverse_row]
    film_out = lax.all_to_all(pieces, "gas", split_axis=1, concat_axis=3, tiled=True)[:, 0]
    cfl = time_step * lax.pmax(peak_speed(film_now), ("wall", "gas"))
    return (film_out, cfl)


def solution(mesh):
    return jax.shard_map(
        per_device,
        mesh=mesh,
        in_specs=(
            P(None, None, "wall", "gas"),
            P("wall", "gas"),
            P(None, "wall", "gas"),
            P("wall", "gas"),
            P(),
        ),
        out_specs=(P(None, ("wall", "gas"), None), P()),
        check_vma=False,
    )
```

profile of v0, /device:TPU:0, one launch (start us, length us, event | category | flops | bytes accessed | tf_op | source)
XLA Modules:
  0.0 186.7 jit_solution(5105787100391867581)
XLA Ops:
  1.5 3.0 %collective-permute-start = (f32[4,1,512]{2,1,0:T(1,128)S(1)}, f32[4,1,512]{2,1,0:T(1,128)S(1)}, u32[]{:S(2)}, u32[]{:S(2)}) collective-permute-start(f32[4,1,512]{2,1,0:T(1,128)S(1)} %get-tuple-element.45), channel_id=1, source_target_pairs={{0,8},{8,16},{16,24},{24,0},{1,9},{9,17},{17,25},{25,1},{2,10},{10... | collective-permute-start | bytes 24584 | tf_op jit(solution)/shard_map/ppermute | solution.py:31
  5.6 2.2 %fusion.10 = f32[3,128,512]{2,1,0:T(8,128)S(1)} fusion(f32[3,4,128,512]{3,2,1,0:T(8,128)} %param.5), kind=kLoop, calls=%fused_computation.48 | loop fusion | flops 1376256 | bytes 3932160 | tf_op jit(solution)/shard_map/add | solution.py:101
  8.9 1.9 %collective-permute-start.5 = (f32[3,1,512]{2,1,0:T(1,128)S(1)}, f32[3,1,512]{2,1,0:T(1,128)S(1)}, u32[]{:S(2)}, u32[]{:S(2)}) collective-permute-start(f32[3,1,512]{2,1,0:T(1,128)S(1)} %get-tuple-element.49), channel_id=1, source_target_pairs={{8,0},{16,8},{24,16},{0,24},{9,1},{17,9},{25,17},{1,25},{10,2},{18... | collective-permute-start | bytes 18440 | tf_op jit(solution)/shard_map/ppermute | solution.py:32
  13.7 3.5 %collective-permute-start.7 = (f32[3,130,1]{2,1,0:T(8,128)}, f32[3,130,1]{2,1,0:T(8,128)}, u32[]{:S(2)}, u32[]{:S(2)}) collective-permute-start(f32[3,130,1]{2,1,0:T(8,128)} %get-tuple-element.47), channel_id=1, source_target_pairs={{1,0},{2,1},{3,2},{4,3},{5,4},{6,5},{7,6},{0,7},{9,8},{10,9},{11,1... | collective-permute-start | bytes 4688 | tf_op jit(solution)/shard_map/ppermute | solution.py:32
  17.3 39.4 %pmax.14 = f32[]{:T(128)} all-reduce(f32[]{:T(128)} %fusion.127), channel_id=1, replica_groups=mesh['wall'=4,'gas'=8] {'wall','gas'}, use_global_device_ids=true, to_apply=%region_1.2 | all-reduce | flops 1 | bytes 8 | tf_op jit(solution)/shard_map/pmax | solution.py:108
  61.0 3.5 %collective-permute-start.3 = (f32[4,130,1]{2,1,0:T(8,128)}, f32[4,130,1]{2,1,0:T(8,128)S(1)}, u32[]{:S(2)}, u32[]{:S(2)}) collective-permute-start(f32[4,130,1]{2,1,0:T(8,128)} %get-tuple-element.31), channel_id=1, source_target_pairs={{1,0},{2,1},{3,2},{4,3},{5,4},{6,5},{7,6},{0,7},{9,8},{10,9},{11,1... | collective-permute-start | bytes 6248 | tf_op jit(solution)/shard_map/ppermute | solution.py:32
  65.1 6.2 %collective-permute-done.2 = f32[4,130,1]{2,1,0:T(8,128)S(1)} collective-permute-done((f32[4,130,1]{2,1,0:T(8,128)}, f32[4,130,1]{2,1,0:T(8,128)S(1)}, u32[]{:S(2)}, u32[]{:S(2)}) %collective-permute-start.2) | collective-permute-done | bytes 2112 | tf_op jit(solution)/shard_map/ppermute | solution.py:31
  74.9 2.3 %collective-permute-start.8 = (f32[4,1,512]{2,1,0:T(1,128)S(1)}, f32[4,1,512]{2,1,0:T(1,128)S(1)}, u32[]{:S(2)}, u32[]{:S(2)}) collective-permute-start(f32[4,1,512]{2,1,0:T(1,128)S(1)} %get-tuple-element.42), channel_id=1, source_target_pairs={{0,8},{8,16},{16,24},{24,0},{1,9},{9,17},{17,25},{25,1},{2,10},{10... | collective-permute-start | bytes 24584 | tf_op jit(solution)/shard_map/ppermute | solution.py:31
  78.5 1.4 collective-permute-done.8
  81.1 3.5 %collective-permute-start.11 = (f32[4,130,1]{2,1,0:T(8,128)S(1)}, f32[4,130,1]{2,1,0:T(8,128)S(1)}, u32[]{:S(2)}, u32[]{:S(2)}) collective-permute-start(f32[4,130,1]{2,1,0:T(8,128)S(1)} %get-tuple-element.27), channel_id=1, source_target_pairs={{1,0},{2,1},{3,2},{4,3},{5,4},{6,5},{7,6},{0,7},{9,8},{10,9},{11,1... | collective-permute-start | bytes 6248 | tf_op jit(solution)/shard_map/ppermute | solution.py:32
  84.9 5.8 %collective-permute-done.10 = f32[4,130,1]{2,1,0:T(8,128)S(1)} collective-permute-done((f32[4,130,1]{2,1,0:T(8,128)S(1)}, f32[4,130,1]{2,1,0:T(8,128)S(1)}, u32[]{:S(2)}, u32[]{:S(2)}) %collective-permute-start.10) | collective-permute-done | bytes 2112 | tf_op jit(solution)/shard_map/ppermute | solution.py:31
  95.0 2.8 %collective-permute-start.12 = (f32[4,1,512]{2,1,0:T(1,128)S(1)}, f32[4,1,512]{2,1,0:T(1,128)S(1)}, u32[]{:S(2)}, u32[]{:S(2)}) collective-permute-start(f32[4,1,512]{2,1,0:T(1,128)S(1)} %get-tuple-element.38), channel_id=1, source_target_pairs={{0,8},{8,16},{16,24},{24,0},{1,9},{9,17},{17,25},{25,1},{2,10},{10... | collective-permute-start | bytes 24584 | tf_op jit(solution)/shard_map/ppermute | solution.py:31
  98.2 1.6 collective-permute-done.12
  99.8 1.7 collective-permute-done.13
  101.7 3.5 %collective-permute-start.15 = (f32[4,130,1]{2,1,0:T(8,128)S(1)}, f32[4,130,1]{2,1,0:T(8,128)S(1)}, u32[]{:S(2)}, u32[]{:S(2)}) collective-permute-start(f32[4,130,1]{2,1,0:T(8,128)S(1)} %get-tuple-element.23), channel_id=1, source_target_pairs={{1,0},{2,1},{3,2},{4,3},{5,4},{6,5},{7,6},{0,7},{9,8},{10,9},{11,1... | collective-permute-start | bytes 6248 | tf_op jit(solution)/shard_map/ppermute | solution.py:32
  105.5 4.3 %collective-permute-done.14 = f32[4,130,1]{2,1,0:T(8,128)S(1)} collective-permute-done((f32[4,130,1]{2,1,0:T(8,128)S(1)}, f32[4,130,1]{2,1,0:T(8,128)S(1)}, u32[]{:S(2)}, u32[]{:S(2)}) %collective-permute-start.14) | collective-permute-done | bytes 2112 | tf_op jit(solution)/shard_map/ppermute | solution.py:31
  112.8 1.6 collective-permute-start.16
  115.8 1.6 collective-permute-done.16
  118.3 3.5 %collective-permute-start.19 = (f32[4,130,1]{2,1,0:T(8,128)S(1)}, f32[4,130,1]{2,1,0:T(8,128)S(1)}, u32[]{:S(2)}, u32[]{:S(2)}) collective-permute-start(f32[4,130,1]{2,1,0:T(8,128)S(1)} %get-tuple-element.19), channel_id=1, source_target_pairs={{1,0},{2,1},{3,2},{4,3},{5,4},{6,5},{7,6},{0,7},{9,8},{10,9},{11,1... | collective-permute-start | bytes 6248 | tf_op jit(solution)/shard_map/ppermute | solution.py:32
  122.1 6.1 %collective-permute-done.18 = f32[4,130,1]{2,1,0:T(8,128)S(1)} collective-permute-done((f32[4,130,1]{2,1,0:T(8,128)S(1)}, f32[4,130,1]{2,1,0:T(8,128)S(1)}, u32[]{:S(2)}, u32[]{:S(2)}) %collective-permute-start.18) | collective-permute-done | bytes 2112 | tf_op jit(solution)/shard_map/ppermute | solution.py:31
  129.6 2.0 %add_reduce_fusion = (f32[]{:T(128)}, f32[128,512]{1,0:T(8,128)S(1)}, f32[128,512]{1,0:T(8,128)S(1)}, f32[128,512]{1,0:T(8,128)S(1)}) fusion(f32[128,512]{1,0:T(8,128)S(1)} %copy-done.2, f32[1,128,512]{2,1,0:T(8,128)S(1)} %bitcast.430, f32[1,128,512]{2,1,0:T(8,128)S(1)} %bitcast.436, f32[1,128,512]{2,1,0:T(8,128)S(1)} %bitcast.442, ...), kind=kLoop, calls=%fused_computation.238 | loop fusion | flops 6881279 | bytes 4280392 | tf_op jit(solution)/shard_map/reduce_max | solution.py:63
  131.6 1.6 gather_fusion
  133.2 3.6 %all-to-all-start = ((f32[4,8,16,512]{3,2,0,1:T(8,128)}), f32[4,8,16,512]{3,2,0,1:T(8,128)S(1)}, u32[]{:S(2)}, u32[]{:S(2)}) async-start(f32[4,8,16,512]{3,2,0,1:T(8,128)} %bitcast.53), calls=%async_computation | async-start | bytes 2097152 | tf_op jit(solution)/shard_map/all_to_all | solution.py:120
  136.8 46.4 %pmax.15 = f32[]{:T(128)} all-reduce(f32[]{:T(128)} %get-tuple-element.2), channel_id=1, replica_groups=mesh['wall'=4,'gas'=8] {'wall','gas'}, use_global_device_ids=true, to_apply=%region_4.5 | all-reduce | flops 1 | bytes 8 | tf_op jit(solution)/shard_map/pmax | solution.py:121
  (90 shorter events, 30.0 us)
Async XLA Ops:
  0.6 16.7 %copy-start = (s32[4,8]{1,0:T(4,128)S(1)}, s32[4,8]{1,0:T(4,128)}, u32[]{:S(2)}) copy-start(s32[4,8]{1,0:T(4,128)} %param.9) | copy-start | bytes 388
  1.5 58.5 %collective-permute-start = (f32[4,1,512]{2,1,0:T(1,128)S(1)}, f32[4,1,512]{2,1,0:T(1,128)S(1)}, u32[]{:S(2)}, u32[]{:S(2)}) collective-permute-start(f32[4,1,512]{2,1,0:T(1,128)S(1)} %get-tuple-element.45), channel_id=1, source_target_pairs={{0,8},{8,16},{16,24},{24,0},{1,9},{9,17},{17,25},{25,1},{2,10},{10... | collective-permute-start | bytes 24584 | tf_op jit(solution)/shard_map/ppermute | solution.py:31
  4.5 6.3 %copy-start.1 = (f32[4,128,512]{2,1,0:T(8,128)S(1)}, f32[4,128,512]{2,1,0:T(8,128)}, u32[]{:S(2)}) copy-start(f32[4,128,512]{2,1,0:T(8,128)} %param.7) | copy-start | bytes 3145732
  4.5 55.6 %collective-permute-start.1 = (f32[4,1,512]{2,1,0:T(1,128)S(1)}, f32[4,1,512]{2,1,0:T(1,128)S(1)}, u32[]{:S(2)}, u32[]{:S(2)}) collective-permute-start(f32[4,1,512]{2,1,0:T(1,128)S(1)} %get-tuple-element.44), channel_id=1, source_target_pairs={{8,0},{16,8},{24,16},{0,24},{9,1},{17,9},{25,17},{1,25},{10,2},{18... | collective-permute-start | bytes 24584 | tf_op jit(solution)/shard_map/ppermute | solution.py:32
  7.8 4.6 %collective-permute-start.4 = (f32[3,1,512]{2,1,0:T(1,128)S(1)}, f32[3,1,512]{2,1,0:T(1,128)S(1)}, u32[]{:S(2)}, u32[]{:S(2)}) collective-permute-start(f32[3,1,512]{2,1,0:T(1,128)S(1)} %get-tuple-element.48), channel_id=1, source_target_pairs={{0,8},{8,16},{16,24},{24,0},{1,9},{9,17},{17,25},{25,1},{2,10},{10... | collective-permute-start | bytes 18440 | tf_op jit(solution)/shard_map/ppermute | solution.py:31
  8.9 4.1 %collective-permute-start.5 = (f32[3,1,512]{2,1,0:T(1,128)S(1)}, f32[3,1,512]{2,1,0:T(1,128)S(1)}, u32[]{:S(2)}, u32[]{:S(2)}) collective-permute-start(f32[3,1,512]{2,1,0:T(1,128)S(1)} %get-tuple-element.49), channel_id=1, source_target_pairs={{8,0},{16,8},{24,16},{0,24},{9,1},{17,9},{25,17},{1,25},{10,2},{18... | collective-permute-start | bytes 18440 | tf_op jit(solution)/shard_map/ppermute | solution.py:32
  10.9 45.8 %copy-start.6 = (s32[128,4]{0,1:T(4,128)S(1)}, s32[128,4]{0,1:T(4,128)}, u32[]{:S(2)}) copy-start(s32[128,4]{0,1:T(4,128)} %param.6) | copy-start | bytes 6148
  13.7 44.7 %collective-permute-start.6 = (f32[3,130,1]{2,1,0:T(8,128)}, f32[3,130,1]{2,1,0:T(8,128)S(1)}, u32[]{:S(2)}, u32[]{:S(2)}) collective-permute-start(f32[3,130,1]{2,1,0:T(8,128)} %get-tuple-element.46), channel_id=1, source_target_pairs={{0,1},{1,2},{2,3},{3,4},{4,5},{5,6},{6,7},{7,0},{8,9},{9,10},{10,1... | collective-permute-start | bytes 4688 | tf_op jit(solution)/shard_map/ppermute | solution.py:31
  13.7 44.8 %collective-permute-start.7 = (f32[3,130,1]{2,1,0:T(8,128)}, f32[3,130,1]{2,1,0:T(8,128)}, u32[]{:S(2)}, u32[]{:S(2)}) collective-permute-start(f32[3,130,1]{2,1,0:T(8,128)} %get-tuple-element.47), channel_id=1, source_target_pairs={{1,0},{2,1},{3,2},{4,3},{5,4},{6,5},{7,6},{0,7},{9,8},{10,9},{11,1... | collective-permute-start | bytes 4688 | tf_op jit(solution)/shard_map/ppermute | solution.py:32
  61.0 10.3 %collective-permute-start.2 = (f32[4,130,1]{2,1,0:T(8,128)}, f32[4,130,1]{2,1,0:T(8,128)S(1)}, u32[]{:S(2)}, u32[]{:S(2)}) collective-permute-start(f32[4,130,1]{2,1,0:T(8,128)} %get-tuple-element.30), channel_id=1, source_target_pairs={{0,1},{1,2},{2,3},{3,4},{4,5},{5,6},{6,7},{7,0},{8,9},{9,10},{10,1... | collective-permute-start | bytes 6248 | tf_op jit(solution)/shard_map/ppermute | solution.py:31
  61.0 10.3 %collective-permute-start.3 = (f32[4,130,1]{2,1,0:T(8,128)}, f32[4,130,1]{2,1,0:T(8,128)S(1)}, u32[]{:S(2)}, u32[]{:S(2)}) collective-permute-start(f32[4,130,1]{2,1,0:T(8,128)} %get-tuple-element.31), channel_id=1, source_target_pairs={{1,0},{2,1},{3,2},{4,3},{5,4},{6,5},{7,6},{0,7},{9,8},{10,9},{11,1... | collective-permute-start | bytes 6248 | tf_op jit(solution)/shard_map/ppermute | solution.py:32
  74.9 5.1 %collective-permute-start.8 = (f32[4,1,512]{2,1,0:T(1,128)S(1)}, f32[4,1,512]{2,1,0:T(1,128)S(1)}, u32[]{:S(2)}, u32[]{:S(2)}) collective-permute-start(f32[4,1,512]{2,1,0:T(1,128)S(1)} %get-tuple-element.42), channel_id=1, source_target_pairs={{0,8},{8,16},{16,24},{24,0},{1,9},{9,17},{17,25},{25,1},{2,10},{10... | collective-permute-start | bytes 24584 | tf_op jit(solution)/shard_map/ppermute | solution.py:31
  77.2 3.7 %collective-permute-start.9 = (f32[4,1,512]{2,1,0:T(1,128)S(1)}, f32[4,1,512]{2,1,0:T(1,128)S(1)}, u32[]{:S(2)}, u32[]{:S(2)}) collective-permute-start(f32[4,1,512]{2,1,0:T(1,128)S(1)} %get-tuple-element.43), channel_id=1, source_target_pairs={{8,0},{16,8},{24,16},{0,24},{9,1},{17,9},{25,17},{1,25},{10,2},{18... | collective-permute-start | bytes 24584 | tf_op jit(solution)/shard_map/ppermute | solution.py:32
  81.0 9.7 %collective-permute-start.10 = (f32[4,130,1]{2,1,0:T(8,128)S(1)}, f32[4,130,1]{2,1,0:T(8,128)S(1)}, u32[]{:S(2)}, u32[]{:S(2)}) collective-permute-start(f32[4,130,1]{2,1,0:T(8,128)S(1)} %get-tuple-element.26), channel_id=1, source_target_pairs={{0,1},{1,2},{2,3},{3,4},{4,5},{5,6},{6,7},{7,0},{8,9},{9,10},{10,1... | collective-permute-start | bytes 6248 | tf_op jit(solution)/shard_map/ppermute | solution.py:31
  81.1 9.6 %collective-permute-start.11 = (f32[4,130,1]{2,1,0:T(8,128)S(1)}, f32[4,130,1]{2,1,0:T(8,128)S(1)}, u32[]{:S(2)}, u32[]{:S(2)}) collective-permute-start(f32[4,130,1]{2,1,0:T(8,128)S(1)} %get-tuple-element.27), channel_id=1, source_target_pairs={{1,0},{2,1},{3,2},{4,3},{5,4},{6,5},{7,6},{0,7},{9,8},{10,9},{11,1... | collective-permute-start | bytes 6248 | tf_op jit(solution)/shard_map/ppermute | solution.py:32
  95.0 4.8 %collective-permute-start.12 = (f32[4,1,512]{2,1,0:T(1,128)S(1)}, f32[4,1,512]{2,1,0:T(1,128)S(1)}, u32[]{:S(2)}, u32[]{:S(2)}) collective-permute-start(f32[4,1,512]{2,1,0:T(1,128)S(1)} %get-tuple-element.38), channel_id=1, source_target_pairs={{0,8},{8,16},{16,24},{24,0},{1,9},{9,17},{17,25},{25,1},{2,10},{10... | collective-permute-start | bytes 24584 | tf_op jit(solution)/shard_map/ppermute | solution.py:31
  97.8 3.7 %collective-permute-start.13 = (f32[4,1,512]{2,1,0:T(1,128)S(1)}, f32[4,1,512]{2,1,0:T(1,128)S(1)}, u32[]{:S(2)}, u32[]{:S(2)}) collective-permute-start(f32[4,1,512]{2,1,0:T(1,128)S(1)} %get-tuple-element.39), channel_id=1, source_target_pairs={{8,0},{16,8},{24,16},{0,24},{9,1},{17,9},{25,17},{1,25},{10,2},{18... | collective-permute-start | bytes 24584 | tf_op jit(solution)/shard_map/ppermute | solution.py:32
  101.6 8.2 %collective-permute-start.14 = (f32[4,130,1]{2,1,0:T(8,128)S(1)}, f32[4,130,1]{2,1,0:T(8,128)S(1)}, u32[]{:S(2)}, u32[]{:S(2)}) collective-permute-start(f32[4,130,1]{2,1,0:T(8,128)S(1)} %get-tuple-element.22), channel_id=1, source_target_pairs={{0,1},{1,2},{2,3},{3,4},{4,5},{5,6},{6,7},{7,0},{8,9},{9,10},{10,1... | collective-permute-start | bytes 6248 | tf_op jit(solution)/shard_map/ppermute | solution.py:31
  101.7 8.1 %collective-permute-start.15 = (f32[4,130,1]{2,1,0:T(8,128)S(1)}, f32[4,130,1]{2,1,0:T(8,128)S(1)}, u32[]{:S(2)}, u32[]{:S(2)}) collective-permute-start(f32[4,130,1]{2,1,0:T(8,128)S(1)} %get-tuple-element.23), channel_id=1, source_target_pairs={{1,0},{2,1},{3,2},{4,3},{5,4},{6,5},{7,6},{0,7},{9,8},{10,9},{11,1... | collective-permute-start | bytes 6248 | tf_op jit(solution)/shard_map/ppermute | solution.py:32
  112.8 4.6 %collective-permute-start.16 = (f32[4,1,512]{2,1,0:T(1,128)S(1)}, f32[4,1,512]{2,1,0:T(1,128)S(1)}, u32[]{:S(2)}, u32[]{:S(2)}) collective-permute-start(f32[4,1,512]{2,1,0:T(1,128)S(1)} %get-tuple-element.34), channel_id=1, source_target_pairs={{0,8},{8,16},{16,24},{24,0},{1,9},{9,17},{17,25},{25,1},{2,10},{10... | collective-permute-start | bytes 24584 | tf_op jit(solution)/shard_map/ppermute | solution.py:31
  114.4 3.7 %collective-permute-start.17 = (f32[4,1,512]{2,1,0:T(1,128)S(1)}, f32[4,1,512]{2,1,0:T(1,128)S(1)}, u32[]{:S(2)}, u32[]{:S(2)}) collective-permute-start(f32[4,1,512]{2,1,0:T(1,128)S(1)} %get-tuple-element.35), channel_id=1, source_target_pairs={{8,0},{16,8},{24,16},{0,24},{9,1},{17,9},{25,17},{1,25},{10,2},{18... | collective-permute-start | bytes 24584 | tf_op jit(solution)/shard_map/ppermute | solution.py:32
  118.2 10.0 %collective-permute-start.18 = (f32[4,130,1]{2,1,0:T(8,128)S(1)}, f32[4,130,1]{2,1,0:T(8,128)S(1)}, u32[]{:S(2)}, u32[]{:S(2)}) collective-permute-start(f32[4,130,1]{2,1,0:T(8,128)S(1)} %get-tuple-element.18), channel_id=1, source_target_pairs={{0,1},{1,2},{2,3},{3,4},{4,5},{5,6},{6,7},{7,0},{8,9},{9,10},{10,1... | collective-permute-start | bytes 6248 | tf_op jit(solution)/shard_map/ppermute | solution.py:31
  118.3 9.9 %collective-permute-start.19 = (f32[4,130,1]{2,1,0:T(8,128)S(1)}, f32[4,130,1]{2,1,0:T(8,128)S(1)}, u32[]{:S(2)}, u32[]{:S(2)}) collective-permute-start(f32[4,130,1]{2,1,0:T(8,128)S(1)} %get-tuple-element.19), channel_id=1, source_target_pairs={{1,0},{2,1},{3,2},{4,3},{5,4},{6,5},{7,6},{0,7},{9,8},{10,9},{11,1... | collective-permute-start | bytes 6248 | tf_op jit(solution)/shard_map/ppermute | solution.py:32
  133.2 50.6 %all-to-all-start = ((f32[4,8,16,512]{3,2,0,1:T(8,128)}), f32[4,8,16,512]{3,2,0,1:T(8,128)S(1)}, u32[]{:S(2)}, u32[]{:S(2)}) async-start(f32[4,8,16,512]{3,2,0,1:T(8,128)} %bitcast.53), calls=%async_computation | async-start | bytes 2097152 | tf_op jit(solution)/shard_map/all_to_all | solution.py:120
  (4 other events, 5.8 us)
where the time goes:
time: 187 us
  blocking collectives  85.8 us (46%)
  starting transfers between devices  38.1 us (20%)
  waiting for transfers between devices  31.5 us (17%)
  other arithmetic  21.3 us (11%)
  local copies, waits for them, and re-layouts  6.58 us (4%)
  between operations  3.49 us (2%)
    pmax x1, blocking collectives, per_device(): cfl = time_step * lax.pmax(peak_speed(film_now), ('wall', 'gas'))  46.4 us
    pmax x1, blocking collectives, per_device(): time_step = COURANT / lax.pmax(peak_speed(film_state), ('wall', 'gas'))  39.4 us
    ppermute x10, waiting for transfers between devices, with_halo(): before = lax.ppermute(last, axis, up)  27.8 us
    ppermute x10, starting transfers between devices, with_halo(): after = lax.ppermute(leading, axis, down)  23.6 us
    ppermute x10, starting transfers between devices, with_halo(): before = lax.ppermute(last, axis, up)  10.9 us
    concatenate x8, other arithmetic, with_halo(): value = jnp.concatenate([before, value, after], axis=dim)  4.46 us
  transfers between devices with their start and end apart: 21, of which 12 were waited for; matrix products, arithmetic and copies ran while one was open for 4% of the time, Pallas kernels for 0%

commit v1 on v0

v1 whole, which is shorter than its diff:
```python
import functools

import jax
import jax.numpy as jnp
from jax import lax
from jax.experimental import pallas as pl
from jax.experimental.pallas import tpu as pltpu
from jax.sharding import PartitionSpec as P

SUBSTEPS = 4
HALO = SUBSTEPS
LANES = 128
SUBLANES = 8

LAYER_WEIGHTS = (0.1, 0.2, 0.3, 0.4)
KAPPA = 0.41
HEIGHT_RATIO = 20.0
SPEED_FLOOR = 0.5
PRANDTL_TURB = 0.85
PRANDTL_JUMP = 3.0
LAMINAR_SHEAR = 0.3
LAMINAR_HEAT = 0.2
FILM_SPREAD = 0.24
FILM_FLOOR = 0.3
FRICTION = 0.5
GRAVITY = 1.0
COURANT = 6.0

FILM, GAS, DEPOSIT, ATTACHED, FIELDS = 0, 4, 7, 8, 9
MESH = pl.DeviceIdType.MESH


def reichardt(scaled_height):
    return jnp.log(1.0 + KAPPA * scaled_height) * (1.0 / KAPPA) + 7.8 * (
        1.0
        - jnp.exp(scaled_height * (-1.0 / 11.0))
        - scaled_height * (1.0 / 11.0) * jnp.exp(scaled_height * (-1.0 / 3.0))
    )


def speed_measure(height, along, across):
    squared = height * height + FILM_FLOOR * FILM_FLOOR
    inverse = lax.rsqrt(squared)
    thickness = squared * inverse
    return jnp.sqrt(along * along + across * across) * inverse + jnp.sqrt(GRAVITY * thickness)


def tile_max(value):
    tiles = [
        value[r : r + SUBLANES, c : c + LANES]
        for r in range(0, value.shape[0], SUBLANES)
        for c in range(0, value.shape[1], LANES)
    ]
    while len(tiles) > 1:
        tiles = [jnp.maximum(a, b) for a, b in zip(tiles[::2], tiles[1::2])] + (
            [tiles[-1]] if len(tiles) % 2 else []
        )
    return tiles[0]


def kernel(
    n_wall, n_gas,
    gas_hbm, flags_hbm, film_hbm, deposit_hbm, owner_hbm,
    out_ref, cfl_ref,
    gas, flags, film, deposit, owner, ext, held, outbox,
    from_north, from_south, east_side, west_side, pack_east, pack_west, corner,
    peak_send, peak_gas, peak_wall,
    load_sem, halo_send, halo_recv, peak_gas_send, peak_gas_recv, peak_wall_send, peak_wall_recv,
    strip_send, strip_recv, own_sem,
):
    rows, cols = film.shape[1], film.shape[2]
    wide = cols + LANES
    strip = rows // n_gas
    block = strip + 2 * HALO
    w, g = lax.axis_index("wall"), lax.axis_index("gas")
    north, south = (w + n_wall - 1) % n_wall, (w + 1) % n_wall
    west, east = (g + n_gas - 1) % n_gas, (g + 1) % n_gas

    loads = [
        pltpu.make_async_copy(film_hbm, film, load_sem.at[0]),
        pltpu.make_async_copy(flags_hbm, flags, load_sem.at[1]),
        pltpu.make_async_copy(deposit_hbm, deposit, load_sem.at[2]),
        pltpu.make_async_copy(owner_hbm, owner, load_sem.at[3]),
    ] + [
        pltpu.make_async_copy(gas_hbm.at[c], gas.at[c], load_sem.at[4 + c]) for c in range(3)
    ]
    for load in loads:
        load.start()

    barrier = pltpu.get_barrier_semaphore()
    peers = (
        [(w, (g + k) % n_gas) for k in range(1, n_gas)]
        + [((w + k) % n_wall, g) for k in range(1, n_wall)]
        + [(a, b) for a in (north, south) for b in (west, east)]
    )
    for peer in peers:
        pl.semaphore_signal(barrier, inc=1, device_id=peer, device_id_type=MESH)

    def gas_peaks(turn):
        return [
            pltpu.make_async_remote_copy(
                src_ref=peak_send.at[turn, 0],
                dst_ref=peak_gas.at[turn, k - 1],
                send_sem=peak_gas_send.at[turn, k - 1],
                recv_sem=peak_gas_recv.at[turn, k - 1],
                device_id=(w, (g + k) % n_gas),
                device_id_type=MESH,
            )
            for k in range(1, n_gas)
        ]

    def wall_peaks(turn):
        return [
            pltpu.make_async_remote_copy(
                src_ref=peak_send.at[turn, 1],
                dst_ref=peak_wall.at[turn, k - 1],
                send_sem=peak_wall_send.at[turn, k - 1],
                recv_sem=peak_wall_recv.at[turn, k - 1],
                device_id=((w + k) % n_wall, g),
                device_id_type=MESH,
            )
            for k in range(1, n_wall)
        ]

    def middle(turn, own_peak, copies):
        for copy in copies:
            copy.wait_recv()
        for k in range(n_gas - 1):
            own_peak = jnp.maximum(own_peak, peak_gas[turn, k])
        peak_send[turn, 1] = own_peak
        later = wall_peaks(turn)
        for copy in later:
            copy.start()
        return later

    def finish(turn, copies):
        for copy in copies:
            copy.wait_recv()
        whole = peak_send[turn, 1]
        for k in range(n_wall - 1):
            whole = jnp.maximum(whole, peak_wall[turn, k])
        return jnp.max(whole)

    loads[0].wait()
    peak_send[0, 0] = tile_max(speed_measure(film[0], film[1], film[2]))
    pl.semaphore_wait(barrier, len(peers))
    first_gas = gas_peaks(0)
    for copy in first_gas:
        copy.start()

    own_rows = slice(HALO, HALO + rows)
    for f in range(4):
        ext[FILM + f, own_rows, 0:cols] = film[f]
    loads[1].wait()
    lane_own = lax.broadcasted_iota(jnp.int32, (rows, LANES), 1)
    for s in range(cols // LANES):
        ext[ATTACHED, own_rows, s * LANES : (s + 1) * LANES] = jnp.where(
            lane_own < flags[:, s : s + 1], 1.0, 0.0
        )
    loads[2].wait()
    ext[DEPOSIT, own_rows, 0:cols] = deposit[...]
    for c in range(3):
        loads[4 + c].wait()
        sampled = LAYER_WEIGHTS[0] * gas[c, 0]
        for layer in range(1, gas.shape[1]):
            sampled = sampled + LAYER_WEIGHTS[layer] * gas[c, layer]
        ext[GAS + c, own_rows, 0:cols] = sampled

    tall = rows + 2 * HALO
    lane = lax.broadcasted_iota(jnp.int32, (tall, LANES), 1)
    to_west = ext[0, :, 0:LANES]
    to_east = pltpu.roll(ext[0, :, cols - LANES : cols], HALO, 1)
    for f in range(1, FIELDS):
        here = lane >= HALO * f
        to_west = jnp.where(here, pltpu.roll(ext[f, :, 0:LANES], HALO * f, 1), to_west)
        to_east = jnp.where(
            here, pltpu.roll(ext[f, :, cols - LANES : cols], HALO * (f + 1), 1), to_east
        )
    pack_west[...] = to_west
    pack_east[...] = to_east

    top, bottom = pl.ds(0, SUBLANES), pl.ds(tall - SUBLANES, SUBLANES)

    def halo(index, src, dst, device):
        return pltpu.make_async_remote_copy(
            src_ref=src, dst_ref=dst, send_sem=halo_send.at[index], recv_sem=halo_recv.at[index],
            device_id=device, device_id_type=MESH,
        )

    halos = [
        halo(0, ext.at[:, top, pl.ds(0, cols)], from_south, (north, g)),
        halo(1, ext.at[:, bottom, pl.ds(0, cols)], from_north, (south, g)),
        halo(2, pack_west, east_side, (w, west)),
        halo(3, pack_east, west_side, (w, east)),
        halo(4, pack_west.at[top], corner.at[0], (north, west)),
        halo(5, pack_west.at[bottom], corner.at[1], (south, west)),
        halo(6, pack_east.at[top], corner.at[2], (north, east)),
        halo(7, pack_east.at[bottom], corner.at[3], (south, east)),
    ]
    for copy in halos:
        copy.start()

    first_wall = middle(0, peak_send[0, 0], first_gas)

    for copy in halos:
        copy.wait()
    for f in range(FIELDS):
        ext[f, 0:HALO, 0:cols] = from_north[f, 0:HALO]
        ext[f, tall - HALO : tall, 0:cols] = from_south[f, HALO : 2 * HALO]
    east_side[tall - HALO : tall] = corner[0, HALO : 2 * HALO]
    east_side[0:HALO] = corner[1, 0:HALO]
    west_side[tall - HALO : tall] = corner[2, HALO : 2 * HALO]
    west_side[0:HALO] = corner[3, 0:HALO]
    for f in range(FIELDS):
        ext[f, :, cols:wide] = jnp.where(
            lane < HALO,
            pltpu.roll(east_side[...], (LANES - HALO * f) % LANES, 1),
            pltpu.roll(west_side[...], LANES - HALO - HALO * f, 1),
        )

    tiles = tall // SUBLANES
    sub = lax.broadcasted_iota(jnp.int32, (SUBLANES, wide), 0)

    def force_tile(i, carry):
        now = pl.ds(pl.multiple_of(i * SUBLANES, SUBLANES), SUBLANES)
        above = pl.ds(pl.multiple_of((i + tiles - 1) % tiles * SUBLANES, SUBLANES), SUBLANES)
        below = pl.ds(pl.multiple_of((i + 1) % tiles * SUBLANES, SUBLANES), SUBLANES)

        def filtered(f):
            centre = ext[f, now, :]
            up = jnp.where(sub == 0, pltpu.roll(ext[f, above, :], 1, 0), pltpu.roll(centre, 1, 0))
            down = jnp.where(
                sub == SUBLANES - 1,
                pltpu.roll(ext[f, below, :], SUBLANES - 1, 0),
                pltpu.roll(centre, SUBLANES - 1, 0),
            )
            total = up + centre + down
            return (pltpu.roll(total, 1, 1) + total + pltpu.roll(total, wide - 1, 1)) * (1.0 / 9.0)

        along, across, gas_heat = filtered(GAS), filtered(GAS + 1), filtered(GAS + 2)
        attached = ext[ATTACHED, now, :] > 0.5
        wall_speed = jnp.sqrt(along * along + across * across + SPEED_FLOOR * SPEED_FLOOR)
        scaled_speed = reichardt(jnp.sqrt(HEIGHT_RATIO * wall_speed))
        contrast = gas_heat - ext[FILM + 3, now, :]
        factor = jnp.where(attached, wall_speed / (scaled_speed * scaled_speed), LAMINAR_SHEAR)
        for f in range(4):
            held[f, i] = ext[FILM + f, now, :]
        held[4, i] = factor * along
        held[5, i] = factor * across
        held[7, i] = ext[DEPOSIT, now, :]
        held[6, i] = contrast * jnp.where(
            attached, wall_speed / (PRANDTL_TURB * scaled_speed + PRANDTL_JUMP), LAMINAR_HEAT
        )
        return carry

    lax.fori_loop(0, tiles, force_tile, 0)

    time_step = COURANT / finish(0, first_wall)
    half = 0.5 * time_step
    loads[3].wait()

    def offset(i):
        return n_gas // 2 + (i + 1) // 2 * (1 - 2 * (i % 2))

    def strip_copy(i):
        return pltpu.make_async_remote_copy(
            src_ref=outbox.at[i],
            dst_ref=out_ref.at[:, :, pl.ds(pl.multiple_of(g * cols, LANES), cols)],
            send_sem=strip_send.at[i],
            recv_sem=strip_recv.at[i],
            device_id=(w, (g + offset(i)) % n_gas),
            device_id_type=MESH,
        )

    def advance_strip(i, peak):
        target = (g + offset(i)) % n_gas
        which = jnp.int32(0)
        for j in range(n_gas):
            match = 1 - jnp.minimum(jnp.abs(owner[w, j] - target), 1)
            which = jnp.maximum(which, j * match)
        first = which * (strip // SUBLANES)

        def window(f):
            return jnp.concatenate([held[f, first + t] for t in range(block // SUBLANES)], axis=0)

        push_along = time_step * window(4)
        push_across = time_step * window(5)
        heating = time_step * window(6)
        spray = time_step * window(7)

        def sides(value):
            return (
                pltpu.roll(value, 1, 0),
                pltpu.roll(value, block - 1, 0),
                pltpu.roll(value, 1, 1),
                pltpu.roll(value, wide - 1, 1),
            )

        def spread(value, n, s, ww, e):
            return (1.0 - 4.0 * FILM_SPREAD) * value + FILM_SPREAD * ((n + s) + (ww + e))

        def substep(_, fields):
            height, along, across, heat = fields
            inverse = lax.rsqrt(height * height + FILM_FLOOR * FILM_FLOOR)
            hn, hs, hw, he = sides(height)
            un, us, uw, ue = sides(along)
            vn, vs, vw, ve = sides(across)
            tn, ts, tw, te = sides(heat)
            drag = (FRICTION * time_step) * inverse
            pull = (GRAVITY * half) * height
            return (
                spread(height, hn, hs, hw, he) + spray - half * ((ue - uw) + (vs - vn)),
                spread(along, un, us, uw, ue) + push_along - drag * along - pull * (he - hw),
                spread(across, vn, vs, vw, ve) + push_across - drag * across - pull * (hs - hn),
                spread(heat, tn, ts, tw, te) + heating * inverse,
            )

        fields = tuple(window(f) for f in range(4))
        fields = lax.fori_loop(0, SUBSTEPS, substep, fields)
        done = [pltpu.roll(value, block - HALO, 0)[0:strip, 0:cols] for value in fields]
        for f in range(4):
            outbox[i, f] = done[f]

        @pl.when(i < n_gas - 1)
        def _():
            strip_copy(i).start()

        return jnp.maximum(peak, tile_max(speed_measure(done[0], done[1], done[2])))

    last_peak = lax.fori_loop(
        0, n_gas, advance_strip, jnp.zeros((SUBLANES, LANES), jnp.float32)
    )
    peak_send[1, 0] = last_peak
    second_gas = gas_peaks(1)
    for copy in second_gas:
        copy.start()
    own = pltpu.make_async_copy(
        outbox.at[n_gas - 1],
        out_ref.at[:, :, pl.ds(pl.multiple_of(g * cols, LANES), cols)],
        own_sem,
    )
    own.start()
    second_wall = middle(1, last_peak, second_gas)
    cfl_ref[0, 0] = time_step * finish(1, second_wall)
    for copy in first_gas + first_wall + second_gas + second_wall:
        copy.wait_send()
    own.wait()
    for i in range(n_gas - 1):
        source = (g + n_gas - offset(i)) % n_gas
        arriving = pltpu.make_async_remote_copy(
            src_ref=outbox.at[i],
            dst_ref=out_ref.at[:, :, pl.ds(pl.multiple_of(source * cols, LANES), cols)],
            send_sem=strip_send.at[i],
            recv_sem=strip_recv.at[i],
            device_id=(w, (g + offset(i)) % n_gas),
            device_id_type=MESH,
        )
        arriving.wait_send()
        arriving.wait_recv()


def per_device(gas_state, wall_flags, film_state, deposit, owner_map):
    n_wall, n_gas = lax.axis_size("wall"), lax.axis_size("gas")
    rows, cols = film_state.shape[1], film_state.shape[2]
    strip = rows // n_gas
    tall, wide = rows + 2 * HALO, cols + LANES
    f32 = jnp.float32
    dma = pltpu.SemaphoreType.DMA
    film_out, cfl = pl.pallas_call(
        functools.partial(kernel, n_wall, n_gas),
        out_shape=(
            jax.ShapeDtypeStruct((4, strip, n_gas * cols), f32),
            jax.ShapeDtypeStruct((1, 1), f32),
        ),
        in_specs=[pl.BlockSpec(memory_space=pl.ANY)] * 5,
        out_specs=(
            pl.BlockSpec(memory_space=pl.ANY),
            pl.BlockSpec(memory_space=pltpu.SMEM),
        ),
        scratch_shapes=[
            pltpu.VMEM(gas_state.shape, f32),
            pltpu.VMEM(wall_flags.shape, jnp.int32),
            pltpu.VMEM(film_state.shape, f32),
            pltpu.VMEM(deposit.shape, f32),
            pltpu.SMEM(owner_map.shape, jnp.int32),
            pltpu.VMEM((FIELDS, tall, wide), f32),
            pltpu.VMEM((8, tall // SUBLANES, SUBLANES, wide), f32),
            pltpu.VMEM((n_gas, 4, strip, cols), f32),
            pltpu.VMEM((FIELDS, SUBLANES, cols), f32),
            pltpu.VMEM((FIELDS, SUBLANES, cols), f32),
            pltpu.VMEM((tall, LANES), f32),
            pltpu.VMEM((tall, LANES), f32),
            pltpu.VMEM((tall, LANES), f32),
            pltpu.VMEM((tall, LANES), f32),
            pltpu.VMEM((4, SUBLANES, LANES), f32),
            pltpu.VMEM((2, 2, SUBLANES, LANES), f32),
            pltpu.VMEM((2, n_gas - 1, SUBLANES, LANES), f32),
            pltpu.VMEM((2, n_wall - 1, SUBLANES, LANES), f32),
            dma((7,)),
            dma((8,)),
            dma((8,)),
            dma((2, n_gas - 1)),
            dma((2, n_gas - 1)),
            dma((2, n_wall - 1)),
            dma((2, n_wall - 1)),
            dma((n_gas - 1,)),
            dma((n_gas - 1,)),
            dma,
        ],
        compiler_params=pltpu.CompilerParams(
            collective_id=0, has_side_effects=True, vmem_limit_bytes=48 * 1024 * 1024
        ),
    )(gas_state, wall_flags, film_state, deposit, owner_map)
    return film_out, cfl.reshape(())


def solution(mesh):
    return jax.shard_map(
        per_device,
        mesh=mesh,
        in_specs=(
            P(None, None, "wall", "gas"),
            P("wall", "gas"),
            P(None, "wall", "gas"),
            P("wall", "gas"),
            P(),
        ),
        out_specs=(P(None, ("wall", "gas"), None), P()),
        check_vma=False,
    )
```

time: 187 us -> 58.4 us (0.31)
  blocking collectives: 85.8 us -> 0 us
  Pallas kernels: 0 us -> 49.3 us
  starting transfers between devices: 38.1 us -> 0 us
  waiting for transfers between devices: 31.5 us -> 0 us
  other arithmetic: 21.3 us -> 0 us
    pmax x2 -> x0, blocking collectives: 85.8 us -> none  [the longest x1 46.4 us: per_device(): cfl = time_step * lax.pmax(peak_speed(film_now), ('wall', 'gas'))]
    pallas_call x0 -> x1, Pallas kernels: none -> 49.3 us  [per_device(): pl.pallas_call(functools.partial(kernel, n_wall, n_gas), out_shape=(jax.S...]
    ppermute x20 -> x0, starting transfers between devices: 34.5 us -> none  [the longest x10 23.6 us: with_halo(): after = lax.ppermute(leading, axis, down)]
    ppermute x20 -> x0, waiting for transfers between devices: 31.5 us -> none  [the longest x10 27.8 us: with_halo(): before = lax.ppermute(last, axis, up)]
    add x14 -> x0, other arithmetic: 8.66 us -> none  [the longest x3 2.24 us: advance(): centre[1] + FILM_SPREAD * spread[1]]
    unnamed x16 -> x10, local copies, waits for them, and re-layouts: 1.18 us -> 6.5 us
    concatenate x8 -> x0, other arithmetic: 4.46 us -> none  [with_halo(): value = jnp.concatenate([before, value, after], axis=dim)]
    all_to_all x1 -> x0, starting transfers between devices: 3.56 us -> none  [per_device(): lax.all_to_all(pieces, 'gas', split_axis=1, concat_axis=3, tiled=True)[:, 0]]
  transfers between devices with their start and end apart: 21 -> 0, of which waited for: 12 -> 0; matrix products, arithmetic and copies ran while one was open for 4% -> 0% of each run, Pallas kernels for 0% -> 0%
where the time goes in v1:
time: 58.4 us; the launch traced here: 58.2 us
  Pallas kernels  49.3 us (84%)
  local copies, waits for them, and re-layouts  6.5 us (11%)
  between operations  2.39 us (4%)
    pallas_call x1, Pallas kernels, per_device(): pl.pallas_call(functools.partial(kernel, n_wall, n_gas), out_shape=(jax.S...  49.3 us
    unnamed x10, local copies, waits for them, and re-layouts  6.5 us

profile of v1, /device:TPU:0, one launch (start us, length us, event | category | flops | bytes accessed | tf_op | source)
XLA Modules:
  0.0 58.2 jit_solution(302875298990580604)
XLA Ops:
  0.6 0.8 %copy.7.flags_hbm = s32[128,4]{1,0:T(8,128)S(1)} copy(s32[128,4]{0,1:T(4,128)} %param.6) | data formatting | bytes 4096 | tf_op args[1]
  1.4 0.0 copy-start
  1.4 1.9 %copy-done = f32[3,4,128,512]{3,2,1,0:T(8,128)S(1)} copy-done((f32[3,4,128,512]{3,2,1,0:T(8,128)S(1)}, f32[3,4,128,512]{3,2,1,0:T(8,128)}, u32[]{:S(2)}) %copy-start) | copy-done | bytes 3145752
  3.3 0.0 copy-start.1
  3.3 1.2 %copy-done.1 = f32[4,128,512]{2,1,0:T(8,128)S(1)} copy-done((f32[4,128,512]{2,1,0:T(8,128)S(1)}, f32[4,128,512]{2,1,0:T(8,128)}, u32[]{:S(2)}) %copy-start.1) | copy-done | bytes 1048600
  4.5 0.0 copy-start.2
  4.5 0.9 %copy-done.2 = f32[128,512]{1,0:T(8,128)S(1)} copy-done((f32[128,512]{1,0:T(8,128)S(1)}, f32[128,512]{1,0:T(8,128)}, u32[]{:S(2)}) %copy-start.2) | copy-done | bytes 262168
  5.5 0.0 copy-start.3
  5.5 0.7 %copy-done.3 = s32[4,8]{1,0:T(4,128)S(1)} copy-done((s32[4,8]{1,0:T(4,128)S(1)}, s32[4,8]{1,0:T(4,128)}, u32[]{:S(2)}) %copy-start.3) | copy-done | bytes 152
  6.2 49.3 %shard_map.68 = (f32[4,16,4096]{2,1,0:T(8,128)S(1)}, f32[1,1]{1,0:T(1,128)}) custom-call(f32[3,4,128,512]{3,2,1,0:T(8,128)S(1)} %copy-done, s32[128,4]{1,0:T(8,128)S(1)} %copy.7.flags_hbm, f32[4,128,512]{2,1,0:T(8,128)S(1)} %copy-done.1, f32[128,512]{1,0:T(8,128)S(1)} %copy-done.2, s32[4,8]{1,0:T(4,128)S(1)} %copy-done.3), custom_call_target="tpu_custom_call" | custom-call | tf_op jit(solution)/shard_map/pallas_call | solution.py:369
  55.4 1.0 %copy.10 = f32[4,16,4096]{2,1,0:T(8,128)} copy(f32[4,16,4096]{2,1,0:T(8,128)S(1)} %get-tuple-element.8) | data formatting | bytes 2097152
Async XLA Ops:
  1.4 1.9 %copy-start = (f32[3,4,128,512]{3,2,1,0:T(8,128)S(1)}, f32[3,4,128,512]{3,2,1,0:T(8,128)}, u32[]{:S(2)}) copy-start(f32[3,4,128,512]{3,2,1,0:T(8,128)} %gas_hbm.1) | copy-start | bytes 9437188
  3.3 1.2 %copy-start.1 = (f32[4,128,512]{2,1,0:T(8,128)S(1)}, f32[4,128,512]{2,1,0:T(8,128)}, u32[]{:S(2)}) copy-start(f32[4,128,512]{2,1,0:T(8,128)} %film_hbm.1) | copy-start | bytes 3145732
  4.5 0.9 %copy-start.2 = (f32[128,512]{1,0:T(8,128)S(1)}, f32[128,512]{1,0:T(8,128)}, u32[]{:S(2)}) copy-start(f32[128,512]{1,0:T(8,128)} %deposit_hbm.1) | copy-start | bytes 786436
  5.5 0.7 %copy-start.3 = (s32[4,8]{1,0:T(4,128)S(1)}, s32[4,8]{1,0:T(4,128)}, u32[]{:S(2)}) copy-start(s32[4,8]{1,0:T(4,128)} %owner_hbm.1) | copy-start | bytes 388

commit v2 on v1

--- a/solution.py
+++ b/solution.py
@@ -63,7 +63,7 @@
     gas_hbm, flags_hbm, film_hbm, deposit_hbm, owner_hbm,
     out_ref, cfl_ref,
     gas, flags, film, deposit, owner, ext, held, outbox,
-    from_north, from_south, east_side, west_side, pack_east, pack_west, corner,
+    from_north, from_south, pack_north, pack_south, east_side, west_side, pack_east, pack_west, corner,
     peak_send, peak_gas, peak_wall,
     load_sem, halo_send, halo_recv, peak_gas_send, peak_gas_recv, peak_wall_send, peak_wall_recv,
     strip_send, strip_recv, own_sem,
@@ -143,19 +143,20 @@
 
     loads[0].wait()
     peak_send[0, 0] = tile_max(speed_measure(film[0], film[1], film[2]))
-    pl.semaphore_wait(barrier, len(peers))
-    first_gas = gas_peaks(0)
-    for copy in first_gas:
-        copy.start()
-
     own_rows = slice(HALO, HALO + rows)
     for f in range(4):
         ext[FILM + f, own_rows, 0:cols] = film[f]
     loads[1].wait()
     lane_own = lax.broadcasted_iota(jnp.int32, (rows, LANES), 1)
-    for s in range(cols // LANES):
+    segments = cols // LANES
+    counts = jnp.concatenate(
+        [flags[...].astype(jnp.float32)] * -(-SUBLANES // segments), axis=0
+    )
+    counts = jnp.concatenate([counts] * (rows // counts.shape[0]), axis=0)
+    counts = jnp.transpose(counts).astype(jnp.int32)
+    for s in range(segments):
         ext[ATTACHED, own_rows, s * LANES : (s + 1) * LANES] = jnp.where(
-            lane_own < flags[:, s : s + 1], 1.0, 0.0
+            lane_own < counts[:, s : s + 1], 1.0, 0.0
         )
     loads[2].wait()
     ext[DEPOSIT, own_rows, 0:cols] = deposit[...]
@@ -178,6 +179,21 @@
         )
     pack_west[...] = to_west
     pack_east[...] = to_east
+    upper = lax.broadcasted_iota(jnp.int32, (SUBLANES, cols), 0) < HALO
+    for f in range(0, FIELDS, 2):
+        low, high = ext[f, 0:SUBLANES, 0:cols], ext[f, tall - SUBLANES : tall, 0:cols]
+        if f + 1 < FIELDS:
+            low = jnp.where(upper, pltpu.roll(ext[f + 1, 0:SUBLANES, 0:cols], HALO, 0), low)
+            high = jnp.where(
+                upper, high, pltpu.roll(ext[f + 1, tall - SUBLANES : tall, 0:cols], HALO, 0)
+            )
+        pack_north[f // 2] = low
+        pack_south[f // 2] = high
+
+    pl.semaphore_wait(barrier, len(peers))
+    first_gas = gas_peaks(0)
+    for copy in first_gas:
+        copy.start()
 
     top, bottom = pl.ds(0, SUBLANES), pl.ds(tall - SUBLANES, SUBLANES)
 
@@ -188,8 +204,8 @@
         )
 
     halos = [
-        halo(0, ext.at[:, top, pl.ds(0, cols)], from_south, (north, g)),
-        halo(1, ext.at[:, bottom, pl.ds(0, cols)], from_north, (south, g)),
+        halo(0, pack_north, from_south, (north, g)),
+        halo(1, pack_south, from_north, (south, g)),
         halo(2, pack_west, east_side, (w, west)),
         halo(3, pack_east, west_side, (w, east)),
         halo(4, pack_west.at[top], corner.at[0], (north, west)),
@@ -203,10 +219,13 @@
     first_wall = middle(0, peak_send[0, 0], first_gas)
 
     for copy in halos:
-        copy.wait()
+        copy.wait_recv()
     for f in range(FIELDS):
-        ext[f, 0:HALO, 0:cols] = from_north[f, 0:HALO]
-        ext[f, tall - HALO : tall, 0:cols] = from_south[f, HALO : 2 * HALO]
+        above, below = from_north[f // 2], from_south[f // 2]
+        if f % 2:
+            above, below = pltpu.roll(above, HALO, 0), pltpu.roll(below, HALO, 0)
+        ext[f, 0:HALO, 0:cols] = above[0:HALO]
+        ext[f, tall - HALO : tall, 0:cols] = below[HALO : 2 * HALO]
     east_side[tall - HALO : tall] = corner[0, HALO : 2 * HALO]
     east_side[0:HALO] = corner[1, 0:HALO]
     west_side[tall - HALO : tall] = corner[2, HALO : 2 * HALO]
@@ -221,10 +240,14 @@
     tiles = tall // SUBLANES
     sub = lax.broadcasted_iota(jnp.int32, (SUBLANES, wide), 0)
 
-    def force_tile(i, carry):
-        now = pl.ds(pl.multiple_of(i * SUBLANES, SUBLANES), SUBLANES)
-        above = pl.ds(pl.multiple_of((i + tiles - 1) % tiles * SUBLANES, SUBLANES), SUBLANES)
-        below = pl.ds(pl.multiple_of((i + 1) % tiles * SUBLANES, SUBLANES), SUBLANES)
+    def tile_rows(i):
+        start = i * SUBLANES
+        return pl.ds(start if isinstance(i, int) else pl.multiple_of(start, SUBLANES), SUBLANES)
+
+    def force_tile(i):
+        now = tile_rows(i)
+        above = tile_rows((i + tiles - 1) % tiles)
+        below = tile_rows((i + 1) % tiles)
 
         def filtered(f):
             centre = ext[f, now, :]
@@ -251,9 +274,15 @@
         held[6, i] = contrast * jnp.where(
             attached, wall_speed / (PRANDTL_TURB * scaled_speed + PRANDTL_JUMP), LAMINAR_HEAT
         )
+
+    def force_pair(i, carry):
+        force_tile(2 * i)
+        force_tile(2 * i + 1)
         return carry
 
-    lax.fori_loop(0, tiles, force_tile, 0)
+    lax.fori_loop(0, tiles // 2, force_pair, 0)
+    if tiles % 2:
+        force_tile(tiles - 1)
 
     time_step = COURANT / finish(0, first_wall)
     half = 0.5 * time_step
@@ -342,7 +371,7 @@
     own.start()
     second_wall = middle(1, last_peak, second_gas)
     cfl_ref[0, 0] = time_step * finish(1, second_wall)
-    for copy in first_gas + first_wall + second_gas + second_wall:
+    for copy in halos + first_gas + first_wall + second_gas + second_wall:
         copy.wait_send()
     own.wait()
     for i in range(n_gas - 1):
@@ -372,22 +401,24 @@
             jax.ShapeDtypeStruct((4, strip, n_gas * cols), f32),
             jax.ShapeDtypeStruct((1, 1), f32),
         ),
-        in_specs=[pl.BlockSpec(memory_space=pl.ANY)] * 5,
+        in_specs=[pl.BlockSpec(memory_space=pltpu.HBM)] * 5,
         out_specs=(
-            pl.BlockSpec(memory_space=pl.ANY),
+            pl.BlockSpec(memory_space=pltpu.HBM),
             pl.BlockSpec(memory_space=pltpu.SMEM),
         ),
         scratch_shapes=[
             pltpu.VMEM(gas_state.shape, f32),
-            pltpu.VMEM(wall_flags.shape, jnp.int32),
+            pltpu.VMEM(wall_flags.shape[::-1], jnp.int32),
             pltpu.VMEM(film_state.shape, f32),
             pltpu.VMEM(deposit.shape, f32),
             pltpu.SMEM(owner_map.shape, jnp.int32),
             pltpu.VMEM((FIELDS, tall, wide), f32),
             pltpu.VMEM((8, tall // SUBLANES, SUBLANES, wide), f32),
             pltpu.VMEM((n_gas, 4, strip, cols), f32),
-            pltpu.VMEM((FIELDS, SUBLANES, cols), f32),
-            pltpu.VMEM((FIELDS, SUBLANES, cols), f32),
+            pltpu.VMEM((-(-FIELDS // 2), SUBLANES, cols), f32),
+            pltpu.VMEM((-(-FIELDS // 2), SUBLANES, cols), f32),
+            pltpu.VMEM((-(-FIELDS // 2), SUBLANES, cols), f32),
+            pltpu.VMEM((-(-FIELDS // 2), SUBLANES, cols), f32),
             pltpu.VMEM((tall, LANES), f32),
             pltpu.VMEM((tall, LANES), f32),
             pltpu.VMEM((tall, LANES), f32),
@@ -408,9 +439,9 @@
             dma,
         ],
         compiler_params=pltpu.CompilerParams(
-            collective_id=0, has_side_effects=True, vmem_limit_bytes=48 * 1024 * 1024
+            collective_id=0, has_side_effects=True, vmem_limit_bytes=60 * 1024 * 1024
         ),
-    )(gas_state, wall_flags, film_state, deposit, owner_map)
+    )(gas_state, wall_flags.T, film_state, deposit, owner_map)
     return film_out, cfl.reshape(())
 
 

time: 58.4 us -> 49.7 us (0.85)
  Pallas kernels: 49.3 us -> 44.9 us
  local copies, waits for them, and re-layouts: 6.5 us -> 2.27 us
    pallas_call x1, Pallas kernels: 49.3 us -> 44.9 us  [per_device(): pl.pallas_call(functools.partial(kernel, n_wall, n_gas), out_shape=(jax.S...]
    unnamed x10 -> x1, local copies, waits for them, and re-layouts: 6.5 us -> 2.27 us
where the time goes in v2:
time: 49.7 us; the launch traced here: 49.5 us
  Pallas kernels  44.9 us (90%)
  between operations  2.33 us (5%)
  local copies, waits for them, and re-layouts  2.27 us (5%)
    pallas_call x1, Pallas kernels, per_device(): pl.pallas_call(functools.partial(kernel, n_wall, n_gas), out_shape=(jax.S...  44.9 us
    unnamed x1, local copies, waits for them, and re-layouts  2.27 us

profile of v2, /device:TPU:0, one launch (start us, length us, event | category | flops | bytes accessed | tf_op | source)
XLA Modules:
  0.0 49.5 jit_solution(4263230144581233243)
XLA Ops:
  0.6 44.9 %shard_map.68 = (f32[4,16,4096]{2,1,0:T(8,128)}, f32[1,1]{1,0:T(1,128)}) custom-call(f32[3,4,128,512]{3,2,1,0:T(8,128)} %gas_hbm.1, s32[4,128]{1,0:T(4,128)} %bitcast.2, f32[4,128,512]{2,1,0:T(8,128)} %film_hbm.1, f32[128,512]{1,0:T(8,128)} %deposit_hbm.1, s32[4,8]{1,0:T(4,128)} %owner_hbm.1), custom_call_target="tpu_custom_call" | custom-call | tf_op jit(solution)/shard_map/pallas_call | solution.py:398
  45.5 2.3 %copy.9 = f32[4,16,4096]{2,1,0:T(8,128)} copy(f32[4,16,4096]{2,1,0:T(8,128)} %get-tuple-element.8) | data formatting | bytes 2097152

commit v3 on v2

--- a/solution.py
+++ b/solution.py
@@ -99,7 +99,7 @@
     def gas_peaks(turn):
         return [
             pltpu.make_async_remote_copy(
-                src_ref=peak_send.at[turn, 0],
+                src_ref=peak_send.at[turn, turn],
                 dst_ref=peak_gas.at[turn, k - 1],
                 send_sem=peak_gas_send.at[turn, k - 1],
                 recv_sem=peak_gas_recv.at[turn, k - 1],
@@ -112,7 +112,7 @@
     def wall_peaks(turn):
         return [
             pltpu.make_async_remote_copy(
-                src_ref=peak_send.at[turn, 1],
+                src_ref=peak_send.at[turn, 1 - turn],
                 dst_ref=peak_wall.at[turn, k - 1],
                 send_sem=peak_wall_send.at[turn, k - 1],
                 recv_sem=peak_wall_recv.at[turn, k - 1],
@@ -122,24 +122,12 @@
             for k in range(1, n_wall)
         ]
 
-    def middle(turn, own_peak, copies):
+    def gather_peaks(turn, own_peak, copies, landed):
         for copy in copies:
             copy.wait_recv()
-        for k in range(n_gas - 1):
-            own_peak = jnp.maximum(own_peak, peak_gas[turn, k])
-        peak_send[turn, 1] = own_peak
-        later = wall_peaks(turn)
-        for copy in later:
-            copy.start()
-        return later
-
-    def finish(turn, copies):
-        for copy in copies:
-            copy.wait_recv()
-        whole = peak_send[turn, 1]
-        for k in range(n_wall - 1):
-            whole = jnp.maximum(whole, peak_wall[turn, k])
-        return jnp.max(whole)
+        for k in range(len(copies)):
+            own_peak = jnp.maximum(own_peak, landed[turn, k])
+        return own_peak
 
     loads[0].wait()
     peak_send[0, 0] = tile_max(speed_measure(film[0], film[1], film[2]))
@@ -216,7 +204,10 @@
     for copy in halos:
         copy.start()
 
-    first_wall = middle(0, peak_send[0, 0], first_gas)
+    peak_send[0, 1] = gather_peaks(0, peak_send[0, 0], first_gas, peak_gas)
+    first_wall = wall_peaks(0)
+    for copy in first_wall:
+        copy.start()
 
     for copy in halos:
         copy.wait_recv()
@@ -284,7 +275,9 @@
     if tiles % 2:
         force_tile(tiles - 1)
 
-    time_step = COURANT / finish(0, first_wall)
+    time_step = COURANT / jnp.max(
+        gather_peaks(0, peak_send[0, 1], first_wall, peak_wall)
+    )
     half = 0.5 * time_step
     loads[3].wait()
 
@@ -360,8 +353,8 @@
         0, n_gas, advance_strip, jnp.zeros((SUBLANES, LANES), jnp.float32)
     )
     peak_send[1, 0] = last_peak
-    second_gas = gas_peaks(1)
-    for copy in second_gas:
+    second_wall = wall_peaks(1)
+    for copy in second_wall:
         copy.start()
     own = pltpu.make_async_copy(
         outbox.at[n_gas - 1],
@@ -369,8 +362,13 @@
         own_sem,
     )
     own.start()
-    second_wall = middle(1, last_peak, second_gas)
-    cfl_ref[0, 0] = time_step * finish(1, second_wall)
+    peak_send[1, 1] = gather_peaks(1, last_peak, second_wall, peak_wall)
+    second_gas = gas_peaks(1)
+    for copy in second_gas:
+        copy.start()
+    cfl_ref[0, 0] = time_step * jnp.max(
+        gather_peaks(1, peak_send[1, 1], second_gas, peak_gas)
+    )
     for copy in halos + first_gas + first_wall + second_gas + second_wall:
         copy.wait_send()
     own.wait()

time: 49.7 us -> 47.3 us (0.952)
  Pallas kernels: 44.9 us -> 42.5 us
    pallas_call x1, Pallas kernels: 44.9 us -> 42.5 us  [per_device(): pl.pallas_call(functools.partial(kernel, n_wall, n_gas), out_shape=(jax.S...]
where the time goes in v3:
time: 47.3 us; the launch traced here: 47.1 us
  Pallas kernels  42.5 us (90%)
  between operations  2.33 us (5%)
  local copies, waits for them, and re-layouts  2.27 us (5%)
    pallas_call x1, Pallas kernels, per_device(): pl.pallas_call(functools.partial(kernel, n_wall, n_gas), out_shape=(jax.S...  42.5 us
    unnamed x1, local copies, waits for them, and re-layouts  2.27 us

profile of v3, /device:TPU:0, one launch (start us, length us, event | category | flops | bytes accessed | tf_op | source)
XLA Modules:
  0.0 47.1 jit_solution(17220182934169002966)
XLA Ops:
  0.6 42.5 %shard_map.68 = (f32[4,16,4096]{2,1,0:T(8,128)}, f32[1,1]{1,0:T(1,128)}) custom-call(f32[3,4,128,512]{3,2,1,0:T(8,128)} %gas_hbm.1, s32[4,128]{1,0:T(4,128)} %bitcast.2, f32[4,128,512]{2,1,0:T(8,128)} %film_hbm.1, f32[128,512]{1,0:T(8,128)} %deposit_hbm.1, s32[4,8]{1,0:T(4,128)} %owner_hbm.1), custom_call_target="tpu_custom_call" | custom-call | tf_op jit(solution)/shard_map/pallas_call | solution.py:396
  43.2 2.3 %copy.9 = f32[4,16,4096]{2,1,0:T(8,128)} copy(f32[4,16,4096]{2,1,0:T(8,128)} %get-tuple-element.8) | data formatting | bytes 2097152
